TPU v7x, 256 devices: a whole 4x4x8 slice. The times are simulated.
256 devices in a mesh: row: 8 (over y, core), col: 32 (over x, z).
Axes of the slice: x: 4, y: 4, z: 8, core: 2. Of those that a mesh axis runs over, the one named last changes fastest.
Arguments:
- initial_warmth: float32 [128, 512, 128], P('row', 'col'), may hold values from -3.5 to 3.5
- substance_factor: float32 [128, 512, 128], P('row', 'col'), may hold values from 1 to 4
Outputs:
- new_temperature: float32 [128, 512, 128], P('row', 'col')
All inputs are finite; a program needn't handle non-finite values.
Results may differ from a plain program's by a relative error of at most 0.00075.
Values sent between devices are 32-bit elements; how exact they have to be, the bound alone decides.
A program may use at most 128 MiB of HBM per device.

v0:
```python
import jax
import jax.numpy as jnp
from jax import lax
from jax.sharding import PartitionSpec as P

lateral = 1500.0
upright_direction = 2.0
warmed_wall_value = 0.5
chilled_wall_value = -0.5
warmth_responsiveness = 0.4


def padded(cells, sides, width):
    for axis, dim in sides:
        count = lax.axis_size(axis)
        ends = count - 1
        head = lax.slice_in_dim(cells, 0, width, axis=dim)
        tail = lax.slice_in_dim(cells, cells.shape[dim] - width, cells.shape[dim], axis=dim)
        cells = jnp.concatenate(
            [
                lax.ppermute(tail, axis, [(i, (i + 1) % count) for i in range(ends)]),
                cells,
                lax.ppermute(head, axis, [((i + 1) % count, i) for i in range(ends)]),
            ],
            axis=dim,
        )
    return cells


def harmonic(one_side, other_side):
    return 2.0 * one_side * other_side / (one_side + other_side)


def shifted_down(values, stride, dimension, filler):
    length = values.shape[dimension]
    pad_shape = list(values.shape)
    pad_shape[dimension] = stride
    padding = jnp.full(pad_shape, filler, values.dtype)
    kept_part = lax.slice_in_dim(values, 0, length - stride, axis=dimension)
    return jnp.concatenate([padding, kept_part], axis=dimension)


def shifted_up(values, stride, dimension, filler):
    length = values.shape[dimension]
    pad_shape = list(values.shape)
    pad_shape[dimension] = stride
    padding = jnp.full(pad_shape, filler, values.dtype)
    kept_part = lax.slice_in_dim(values, stride, length, axis=dimension)
    return jnp.concatenate([kept_part, padding], axis=dimension)


def cyclic_reduce(low_band, main_band, high_band, columns, dimension):
    length = main_band.shape[dimension]
    stride = 1
    while stride < length:
        left_factor = -low_band / shifted_down(main_band, stride, dimension, 1.0)
        right_factor = -high_band / shifted_up(main_band, stride, dimension, 1.0)
        new_main = (
            main_band
            + left_factor * shifted_down(high_band, stride, dimension, 0.0)
            + right_factor * shifted_up(low_band, stride, dimension, 0.0)
        )
        new_low = left_factor * shifted_down(low_band, stride, dimension, 0.0)
        new_high = right_factor * shifted_up(high_band, stride, dimension, 0.0)
        columns = [
            column
            + left_factor * shifted_down(column, stride, dimension, 0.0)
            + right_factor * shifted_up(column, stride, dimension, 0.0)
            for column in columns
        ]
        main_band, low_band, high_band = (new_main, new_low, new_high)
        stride = stride * 2
    return [column / main_band for column in columns]


def local_blocks(side, low_band, main_band, high_band, dimension):
    length = main_band.shape[dimension]
    position = lax.broadcasted_iota(jnp.int32, main_band.shape, dimension)
    at_first = position == 0
    at_last = position == length - 1
    inner_low = jnp.where(at_first, 0.0, low_band)
    inner_high = jnp.where(at_last, 0.0, high_band)
    left_side = jnp.where(at_first, low_band, 0.0)
    right_side = jnp.where(at_last, high_band, 0.0)
    solved, left_part, right_part = cyclic_reduce(
        inner_low, main_band, inner_high, [side, left_side, right_side], dimension
    )

    def first_row(values):
        return lax.index_in_dim(values, 0, dimension, keepdims=False)

    def last_row(values):
        return lax.index_in_dim(values, length - 1, dimension, keepdims=False)

    stacked = jnp.stack(
        [
            first_row(left_part),
            last_row(left_part),
            first_row(right_part),
            last_row(right_part),
            first_row(solved),
            last_row(solved),
        ]
    )
    return (solved, left_part, right_part, stacked.reshape(6, -1))


def combine_blocks(solved, left_part, right_part, prev_last, next_first, dimension):
    edge_shape = list(solved.shape)
    edge_shape[dimension] = 1
    return (
        solved
        - left_part * prev_last.reshape(edge_shape)
        - right_part * next_first.reshape(edge_shape)
    )


def mat_mul(first, second):
    return (
        first[0] * second[0] + first[1] * second[2],
        first[0] * second[1] + first[1] * second[3],
        first[2] * second[0] + first[3] * second[2],
        first[2] * second[1] + first[3] * second[3],
    )


def mat_vec(first, vector):
    return (
        first[0] * vector[0] + first[1] * vector[1],
        first[2] * vector[0] + first[3] * vector[1],
    )


def mat_inverse(first):
    determinant = first[0] * first[3] - first[1] * first[2]
    return (
        first[3] / determinant,
        -first[1] / determinant,
        -first[2] / determinant,
        first[0] / determinant,
    )


def shift_tuple(values, stride, downward, fillers):
    if downward:
        return tuple(
            (shifted_down(value, stride, 0, filler) for value, filler in zip(values, fillers))
        )
    return tuple((shifted_up(value, stride, 0, filler) for value, filler in zip(values, fillers)))


def solve_chain(coeffs):
    blank = jnp.zeros_like(coeffs[:, 0])
    unity = jnp.ones_like(coeffs[:, 0])
    lower_mat = (blank, coeffs[:, 0], blank, coeffs[:, 1])
    upper_mat = (coeffs[:, 2], blank, coeffs[:, 3], blank)
    diag_mat = (unity, blank, blank, unity)
    rhs_vec = (coeffs[:, 4], coeffs[:, 5])
    count = coeffs.shape[0]
    zeros4 = (0.0, 0.0, 0.0, 0.0)
    ident4 = (1.0, 0.0, 0.0, 1.0)
    stride = 1
    while stride < count:
        diag_below = shift_tuple(diag_mat, stride, True, ident4)
        diag_above = shift_tuple(diag_mat, stride, False, ident4)
        alpha = mat_mul(lower_mat, mat_inverse(diag_below))
        alpha = tuple((-value for value in alpha))
        beta = mat_mul(upper_mat, mat_inverse(diag_above))
        beta = tuple((-value for value in beta))
        upper_below = shift_tuple(upper_mat, stride, True, zeros4)
        lower_above = shift_tuple(lower_mat, stride, False, zeros4)
        lower_below = shift_tuple(lower_mat, stride, True, zeros4)
        upper_above = shift_tuple(upper_mat, stride, False, zeros4)
        rhs_below = shift_tuple(rhs_vec, stride, True, (0.0, 0.0))
        rhs_above = shift_tuple(rhs_vec, stride, False, (0.0, 0.0))
        term_one = mat_mul(alpha, upper_below)
        term_two = mat_mul(beta, lower_above)
        diag_mat = tuple((d + a + b for d, a, b in zip(diag_mat, term_one, term_two)))
        new_lower = mat_mul(alpha, lower_below)
        new_upper = mat_mul(beta, upper_above)
        add_one = mat_vec(alpha, rhs_below)
        add_two = mat_vec(beta, rhs_above)
        rhs_vec = tuple((r + a + b for r, a, b in zip(rhs_vec, add_one, add_two)))
        lower_mat, upper_mat = (new_lower, new_upper)
        stride = stride * 2
    firsts, lasts = mat_vec(mat_inverse(diag_mat), rhs_vec)
    prev_last = shifted_down(lasts, 1, 0, 0.0)
    next_first = shifted_up(firsts, 1, 0, 0.0)
    return (prev_last, next_first)


def settle_y(packed):
    everyone = lax.all_gather(packed[None], "col", axis=0, tiled=True)
    prev_last, next_first = solve_chain(everyone)
    own_index = lax.axis_index("col")
    return (
        lax.dynamic_index_in_dim(prev_last, own_index, 0, keepdims=False),
        lax.dynamic_index_in_dim(next_first, own_index, 0, keepdims=False),
    )


def settle_x(packed):
    everyone = lax.all_gather(packed[None], "row", axis=0, tiled=True)
    prev_last, next_first = solve_chain(everyone)
    own_index = lax.axis_index("row")
    return (
        lax.dynamic_index_in_dim(prev_last, own_index, 0, keepdims=False),
        lax.dynamic_index_in_dim(next_first, own_index, 0, keepdims=False),
    )


def shards(initial_warmth, substance_factor):
    diffusivity_scale = substance_factor * (1.0 + warmth_responsiveness * jnp.tanh(initial_warmth))
    bordered_array = padded(
        jnp.stack([initial_warmth, diffusivity_scale]), (("row", 1), ("col", 2)), 1
    )
    warmth_bordered_crosswise = bordered_array[0, :, 1:-1, :]
    cond_wide_x = bordered_array[1, :, 1:-1, :]
    warmth_bordered_spanwise = bordered_array[0, 1:-1, :, :]
    cond_wide_y = bordered_array[1, 1:-1, :, :]
    crosswise_interfaces = harmonic(cond_wide_x[:-1], cond_wide_x[1:])
    spanwise_interfaces = harmonic(cond_wide_y[:, :-1], cond_wide_y[:, 1:])
    inner_z = harmonic(diffusivity_scale[:, :, :-1], diffusivity_scale[:, :, 1:])
    gravity_interfaces = jnp.concatenate(
        [diffusivity_scale[:, :, :1], inner_z, diffusivity_scale[:, :, -1:]], axis=2
    )
    energy_current_crosswise = crosswise_interfaces[1:] * (
        warmth_bordered_crosswise[2:] - initial_warmth
    ) - crosswise_interfaces[:-1] * (initial_warmth - warmth_bordered_crosswise[:-2])
    energy_current_spanwise = spanwise_interfaces[:, 1:] * (
        warmth_bordered_spanwise[:, 2:] - initial_warmth
    ) - spanwise_interfaces[:, :-1] * (initial_warmth - warmth_bordered_spanwise[:, :-2])
    beneath_adjacent_volumes = jnp.concatenate(
        [jnp.full_like(initial_warmth[:, :, :1], warmed_wall_value), initial_warmth[:, :, :-1]],
        axis=2,
    )
    overhead_adjacent_volumes = jnp.concatenate(
        [initial_warmth[:, :, 1:], jnp.full_like(initial_warmth[:, :, :1], chilled_wall_value)],
        axis=2,
    )
    energy_current_gravity = gravity_interfaces[:, :, 1:] * (
        overhead_adjacent_volumes - initial_warmth
    ) - gravity_interfaces[:, :, :-1] * (initial_warmth - beneath_adjacent_volumes)
    explicit_rhs = 2.0 * (
        lateral * energy_current_crosswise
        + lateral * energy_current_spanwise
        + upright_direction * energy_current_gravity
    )
    elevation_coordinate = lax.broadcasted_iota(jnp.int32, initial_warmth.shape, 2)
    low_z = jnp.where(
        elevation_coordinate == 0, 0.0, -upright_direction * gravity_interfaces[:, :, :-1]
    )
    upper_height = jnp.where(
        elevation_coordinate == initial_warmth.shape[2] - 1,
        0.0,
        -upright_direction * gravity_interfaces[:, :, 1:],
    )
    main_z = 1.0 + upright_direction * (
        gravity_interfaces[:, :, :-1] + gravity_interfaces[:, :, 1:]
    )
    first_section = cyclic_reduce(low_z, main_z, upper_height, [explicit_rhs], 2)[0]
    minus_y = spanwise_interfaces[:, :-1]
    plus_y = spanwise_interfaces[:, 1:]
    main_y = 1.0 + lateral * (minus_y + plus_y)
    solved, left_part, right_part, packed = local_blocks(
        first_section, -lateral * minus_y, main_y, -lateral * plus_y, 1
    )
    prev_last, next_first = settle_y(packed)
    second_section = combine_blocks(solved, left_part, right_part, prev_last, next_first, 1)
    minus_x = crosswise_interfaces[:-1]
    plus_x = crosswise_interfaces[1:]
    main_x = 1.0 + lateral * (minus_x + plus_x)
    solved, left_part, right_part, packed = local_blocks(
        second_section, -lateral * minus_x, main_x, -lateral * plus_x, 0
    )
    prev_last, next_first = settle_x(packed)
    closing_portion = combine_blocks(solved, left_part, right_part, prev_last, next_first, 0)
    return initial_warmth + closing_portion


def solution(mesh):
    return jax.shard_map(
        shards,
        mesh=mesh,
        in_specs=(P("row", "col", None), P("row", "col", None)),
        out_specs=P("row", "col", None),
        check_vma=False,
    )
```

profile of v0, /device:TPU:1, one launch (start us, length us, event | category | flops | bytes accessed | tf_op | source)
XLA Modules:
  0.0 168.1 jit_solution(7931087927044257494)
XLA Ops:
  6.5 1.0 add_multiply_fusion
  7.6 0.7 pad_maximum_fusion.13
  8.3 4.6 %collective-permute-start = (f32[2,1,16,128]{3,2,1,0:T(8,128)S(1)}, f32[2,1,16,128]{3,2,1,0:T(8,128)S(1)}, u32[]{:S(2)}, u32[]{:S(2)}) collective-permute-start(f32[2,1,16,128]{3,2,1,0:T(8,128)S(1)} %get-tuple-element.366), channel_id=1, source_target_pairs={{0,32},{32,64},{64,96},{96,128},{128,160},{160,192},{192,224},{1,3... | collective-permute-start | bytes 49160 | tf_op jit(solution)/shard_map/ppermute | solution.py:21
  12.9 1.9 %collective-permute-start.1 = (f32[2,1,16,128]{3,2,1,0:T(8,128)S(1)}, f32[2,1,16,128]{3,2,1,0:T(8,128)S(1)}, u32[]{:S(2)}, u32[]{:S(2)}) collective-permute-start(f32[2,1,16,128]{3,2,1,0:T(8,128)S(1)} %get-tuple-element.367), channel_id=1, source_target_pairs={{32,0},{64,32},{96,64},{128,96},{160,128},{192,160},{224,192},{33,... | collective-permute-start | bytes 49160 | tf_op jit(solution)/shard_map/ppermute | solution.py:23
  14.8 1.1 fusion.269
  16.4 1.5 collective-permute-done.1
  18.0 1.3 collective-permute-start.3
  19.3 4.2 %collective-permute-start.2 = (f32[2,18,1,128]{3,2,1,0:T(1,128)S(1)}, f32[2,18,1,128]{3,2,1,0:T(1,128)S(1)}, u32[]{:S(2)}, u32[]{:S(2)}) collective-permute-start(f32[2,18,1,128]{3,2,1,0:T(1,128)S(1)} %get-tuple-element.219), channel_id=1, source_target_pairs={{0,1},{1,2},{2,3},{3,4},{4,5},{5,6},{6,7},{7,8},{8,9},{9,10},{10,1... | collective-permute-start | bytes 55304 | tf_op jit(solution)/shard_map/ppermute | solution.py:21
  23.6 0.8 collective-permute-done.2
  31.7 0.7 stack.36
  32.6 78.0 %all-gather.2.cloned.1.call-done = f32[32,6,2048]{2,1,0:T(8,128)} async-done(((f32[1,6,2048]{2,1,0:T(8,128)}), f32[32,6,2048]{2,1,0:T(8,128)}) %all-gather.2.cloned.1.call-update) | async-done | bytes 1572880 | tf_op jit(solution)/shard_map/all_gather | solution.py:193
  110.6 13.0 %fusion.180 = (f32[31,1,2048]{2,1,0:T(1,128)S(1)}, f32[31,1,2048]{2,1,0:T(1,128)S(1)}, f32[31,1,2048]{2,1,0:T(1,128)S(1)}, f32[31,1,2048]{2,1,0:T(1,128)S(1)}, f...) fusion(f32[32,6,2048]{2,1,0:T(8,128)} %all-gather.2.cloned.1.ca, ...), kind=kLoop, calls=%fused_computation.687 | loop fusion | bytes 6094848 | tf_op jit(solution)/shard_map/slice | solution.py:48
  124.3 0.9 copy-done.1
  125.2 1.1 fusion.181
  126.3 0.5 fusion.82
  126.8 0.8 fusion.73
  128.4 0.6 multiply_add_fusion.10
  129.1 0.5 add_add_fusion.2
  130.1 0.4 add_add_fusion.10
  130.6 0.5 add_add_fusion.3
  131.9 0.5 add_add_fusion.7
  132.4 0.4 multiply_add_fusion.2
  134.5 0.3 fusion.5
  135.3 0.3 fusion.32
  135.7 0.3 fusion.18
  136.3 0.7 copy-done.3
  137.1 0.8 multiply_subtract_fusion
  139.6 17.8 %all_gather.7 = f32[8,6,2048]{2,1,0:T(8,128)S(1)} all-gather(f32[1,6,2048]{2,1,0:T(8,128)S(1)} %broadcast_in_dim_reshape.4), channel_id=1, replica_groups=mesh['row'=8,'col'=32] {'row'}, dimensions={0}, use_global_device_ids=true | all-gather | bytes 442368 | tf_op jit(solution)/shard_map/all_gather | solution.py:203
  157.4 0.4 fusion.183
  157.8 0.3 fusion.182
  160.1 0.3 multiply_subtract_fusion.6
  160.5 0.7 subtract_add_fusion
  (274 shorter events, 15.5 us)
Async XLA Ops:
  6.5 11.4 %copy-start = (f32[16,16,128]{2,1,0:T(8,128)S(1)}, f32[16,16,128]{2,1,0:T(8,128)}, u32[]{:S(2)}) copy-start(f32[16,16,128]{2,1,0:T(8,128)} %param.2) | copy-start | bytes 393220
  6.5 104.0 %all-gather.2.cloned.1.call-start = ((), (), s32[]{:S(2)}) async-start(), calls=%async_computation | async-start | bytes 2162688 | tf_op jit(solution)/shard_map/all_gather | solution.py:193
  8.3 8.1 %collective-permute-start = (f32[2,1,16,128]{3,2,1,0:T(8,128)S(1)}, f32[2,1,16,128]{3,2,1,0:T(8,128)S(1)}, u32[]{:S(2)}, u32[]{:S(2)}) collective-permute-start(f32[2,1,16,128]{3,2,1,0:T(8,128)S(1)} %get-tuple-element.366), channel_id=1, source_target_pairs={{0,32},{32,64},{64,96},{96,128},{128,160},{160,192},{192,224},{1,3... | collective-permute-start | bytes 49160 | tf_op jit(solution)/shard_map/ppermute | solution.py:21
  12.9 5.1 %collective-permute-start.1 = (f32[2,1,16,128]{3,2,1,0:T(8,128)S(1)}, f32[2,1,16,128]{3,2,1,0:T(8,128)S(1)}, u32[]{:S(2)}, u32[]{:S(2)}) collective-permute-start(f32[2,1,16,128]{3,2,1,0:T(8,128)S(1)} %get-tuple-element.367), channel_id=1, source_target_pairs={{32,0},{64,32},{96,64},{128,96},{160,128},{192,160},{224,192},{33,... | collective-permute-start | bytes 49160 | tf_op jit(solution)/shard_map/ppermute | solution.py:23
  18.0 5.6 %collective-permute-start.3 = (f32[2,18,1,128]{3,2,1,0:T(1,128)S(1)}, f32[2,18,1,128]{3,2,1,0:T(1,128)S(1)}, u32[]{:S(2)}, u32[]{:S(2)}) collective-permute-start(f32[2,18,1,128]{3,2,1,0:T(1,128)S(1)} %get-tuple-element.220), channel_id=1, source_target_pairs={{1,0},{2,1},{3,2},{4,3},{5,4},{6,5},{7,6},{8,7},{9,8},{10,9},{11,1... | collective-permute-start | bytes 55304 | tf_op jit(solution)/shard_map/ppermute | solution.py:23
  19.3 5.0 %collective-permute-start.2 = (f32[2,18,1,128]{3,2,1,0:T(1,128)S(1)}, f32[2,18,1,128]{3,2,1,0:T(1,128)S(1)}, u32[]{:S(2)}, u32[]{:S(2)}) collective-permute-start(f32[2,18,1,128]{3,2,1,0:T(1,128)S(1)} %get-tuple-element.219), channel_id=1, source_target_pairs={{0,1},{1,2},{2,3},{3,4},{4,5},{5,6},{6,7},{7,8},{8,9},{9,10},{10,1... | collective-permute-start | bytes 55304 | tf_op jit(solution)/shard_map/ppermute | solution.py:21
  123.6 1.6 copy-start.1
  135.3 0.8 copy-start.2
  136.1 1.0 copy-start.3
  136.1 1.0 slice-start
Sparse Core Ops, SparseCore 0:
  32.5 77.9 all-gather.1
where the time goes:
time: 168 us
  waiting for transfers between devices  80.3 us (48%)
  local copies, waits for them, and re-layouts  24.9 us (15%)
  blocking collectives  17.8 us (11%)
  other arithmetic  17.6 us (10%)
  between operations  15.5 us (9%)
  starting transfers between devices  12 us (7%)
    all_gather x1, waiting for transfers between devices, settle_y(): everyone = lax.all_gather(packed[None], 'col', axis=0, tiled=True)  78 us
    all_gather x1, blocking collectives, settle_x(): everyone = lax.all_gather(packed[None], 'row', axis=0, tiled=True)  17.8 us
    slice x67, local copies, waits for them, and re-layouts, shifted_up(): kept_part = lax.slice_in_dim(values, stride, length, axis=dimension)  15.3 us
    ppermute x2, starting transfers between devices, padded(): lax.ppermute(tail, axis, [(i, (i + 1) % count) for i in range(ends)])  8.75 us
  transfers between devices with their start and end apart: 5, of which 3 were waited for; matrix products, arithmetic and copies ran while one was open for 1% of the time, Pallas kernels for 0%

commit v1 on v0

v1 whole, which is shorter than its diff:
```python
import functools

import jax
import jax.numpy as jnp
from jax import lax
from jax.experimental import pallas as pl
from jax.experimental.pallas import tpu as pltpu
from jax.sharding import PartitionSpec as P

MESH = pl.DeviceIdType.MESH
LATERAL = 1500.0
UPRIGHT = 2.0
WARM_WALL = 0.5
CHILL_WALL = -0.5
RESPONSE = 0.4
B = 16
NZ = 128
ROWS = 8
GROUP = 8
GROUPS = 4
STEPS = (1, 2, 4, 8, 16, 32, 64)


def inverse(value):
    guess = pl.reciprocal(value, approx=True)
    return guess * (2.0 - value * guess)


def conductivity(temperature, factor):
    return factor * (1.0 + RESPONSE * jnp.tanh(temperature))


def half_resistance(conduct):
    return inverse((2.0 * LATERAL) * conduct)


def block_coefficients(half, link, back, green_first, green_last, out):
    left = jnp.ones((B, NZ), jnp.float32)
    right = jnp.ones((B, NZ), jnp.float32)
    lefts, rights = {}, {}
    for step in range(1, B):
        i, j = step, B - step
        resist = half[i - 1] + half[i]
        lefts[i] = inverse(1.0 + left * resist)
        link[i] = lefts[i]
        back[i] = lefts[i] * resist
        left = 1.0 + left * lefts[i]
        resist = half[j - 1] + half[j]
        rights[j] = inverse(1.0 + right * resist)
        right = 1.0 + right * rights[j]
    first, last = inverse(right), inverse(left)
    out[0] = first + half[0]
    out[1] = last + half[B - 1]
    green_first[0] = first
    green_last[B - 1] = last
    for i in range(1, B):
        first = first * rights[i]
        green_first[i] = first
        last = last * lefts[B - i]
        green_last[B - 1 - i] = last
    out[2] = first


def block_ends(load, green_first, green_last, out):
    firsts = [None] * 4
    lasts = [None] * 4
    for i in range(B):
        value = load(i)
        a, b = green_first[i] * value, green_last[i] * value
        k = i % 4
        firsts[k] = a if firsts[k] is None else firsts[k] + a
        lasts[k] = b if lasts[k] is None else lasts[k] + b
    out[0] = (firsts[0] + firsts[1]) + (firsts[2] + firsts[3])
    out[1] = (lasts[0] + lasts[1]) + (lasts[2] + lasts[3])


def block_solve(load, store, link, back, green_last):
    values = [load(0)]
    for i in range(1, B):
        values.append(load(i) + link[i] * values[-1])
    solved = values[-1] * green_last[B - 1]
    store(B - 1, solved)
    for i in range(B - 1, 0, -1):
        solved = back[i] * values[i - 1] + link[i] * solved
        store(i - 1, solved)


def chain_factors(count, coeffs, link, inv, carry):
    previous = None
    for i in range(1, count):
        pivot = coeffs[i - 1, 1] + coeffs[i, 0]
        if previous is not None:
            link[i] = coeffs[i - 1, 2] * previous
            pivot = pivot - coeffs[i - 1, 2] * link[i]
        previous = inverse(pivot)
        inv[i] = previous
        carry[i] = coeffs[i, 2] * previous


def chain_solve(count, ends, link, inv, carry, out):
    values = [None, ends[1, 0] - ends[0, 1]]
    for i in range(2, count):
        values.append((ends[i, 0] - ends[i - 1, 1]) + link[i] * values[-1])
    flux = values[count - 1] * inv[count - 1]
    out[count - 1] = flux
    for i in range(count - 2, 0, -1):
        flux = values[i] * inv[i] + carry[i] * flux
        out[i] = flux


def group_coefficients(coeffs, link, inv, carry, from_left, from_right, out):
    n = GROUP
    zero = jnp.zeros((B, NZ), jnp.float32)
    one = jnp.ones((B, NZ), jnp.float32)
    flux = carry[n - 1]
    from_right[n] = one
    from_right[0] = zero
    from_right[n - 1] = flux
    out[1] = coeffs[n - 1, 1] - coeffs[n - 1, 2] * flux
    for i in range(n - 2, 0, -1):
        flux = carry[i] * flux
        from_right[i] = flux
    out[2] = coeffs[0, 2] * flux
    values = [None, coeffs[0, 2]]
    for i in range(2, n):
        values.append(link[i] * values[-1])
    flux = values[n - 1] * inv[n - 1]
    from_left[0] = one
    from_left[n] = zero
    from_left[n - 1] = flux
    for i in range(n - 2, 0, -1):
        flux = values[i] * inv[i] + carry[i] * flux
        from_left[i] = flux
    out[0] = coeffs[0, 0] - coeffs[0, 2] * flux


def up(value, stride):
    return pltpu.roll(value, stride, axis=1)


def down(value, stride):
    return pltpu.roll(value, NZ - stride, axis=1)


def upright_bands(conduct, lane):
    below = up(conduct, 1)
    face = (2.0 * conduct * below) * inverse(conduct + below)
    inner = jnp.where(lane == 0, 0.0, UPRIGHT * face)
    wall = jnp.where((lane == 0) | (lane == NZ - 1), UPRIGHT * conduct, 0.0)
    main = 1.0 + inner + down(inner, 1) + wall
    return inner, main


def upright_step(link, main, stride):
    inv = inverse(main)
    low = link * up(inv, stride)
    high = link * inv
    new_main = main - low * link - down(high * link, stride)
    return low, high, low * up(link, stride), new_main


def kernel(
    warmth_hbm,
    factor_hbm,
    out_ref,
    warmth,
    factor,
    half_x,
    warmth_t,
    conduct_t,
    half_y,
    side_t,
    side_n,
    halo,
    low_f,
    high_f,
    scale_f,
    link_x,
    back_x,
    gf_x,
    gl_x,
    link_y,
    back_y,
    gf_y,
    gl_y,
    solved,
    co_z,
    co_x,
    co_r,
    end_z,
    end_x,
    end_r,
    ch_link,
    ch_inv,
    ch_carry,
    flux_z,
    flux_x,
    flux_r,
    from_left,
    from_right,
    load_sem,
    send_sem,
    recv_sem,
):
    row = lax.axis_index("row")
    col = lax.axis_index("col")
    me_x = col // GROUP
    me_z = lax.rem(col, GROUP)
    base = me_x * GROUP

    far_first = (4, 3, 5, 2, 6, 1, 7)
    z_peers = [(row, base + lax.rem(me_z + k, GROUP)) for k in far_first]
    x_peers = [(row, lax.rem(col + GROUP * k, GROUP * GROUPS)) for k in (2, 1, 3)]
    row_peers = [(lax.rem(row + k, ROWS), col) for k in far_first]
    columns = GROUP * GROUPS
    row_up, row_down = (lax.rem(row + 1, ROWS), col), (lax.rem(row + ROWS - 1, ROWS), col)
    col_up, col_down = (row, lax.rem(col + 1, columns)), (row, lax.rem(col + columns - 1, columns))

    barrier = pltpu.get_barrier_semaphore()
    everyone = [col_up, col_down] + row_peers + z_peers + x_peers
    for peer in everyone:
        pl.semaphore_signal(barrier, inc=1, device_id=peer, device_id_type=MESH)
    load_w = pltpu.make_async_copy(warmth_hbm, warmth, load_sem.at[0])
    load_f = pltpu.make_async_copy(factor_hbm, factor, load_sem.at[1])
    load_w.start()
    load_f.start()
    pl.semaphore_wait(barrier, len(everyone))

    def remote(src, dst, which, peer):
        return pltpu.make_async_remote_copy(
            src_ref=src,
            dst_ref=dst,
            send_sem=send_sem.at[which],
            recv_sem=recv_sem.at[which],
            device_id=peer,
            device_id_type=MESH,
        )

    for k, array in enumerate((warmth_hbm, factor_hbm)):
        remote(array.at[:, B - 1, :], halo.at[4 + k], 0, col_up).start()
        remote(array.at[:, 0, :], halo.at[6 + k], 0, col_down).start()
        remote(array.at[B - 1], halo.at[k], 0, row_up).start()
        remote(array.at[0], halo.at[2 + k], 0, row_down).start()

    def settle(buffer, count, sem):
        view = buffer.at[pl.ds(0, count)]
        pltpu.make_async_copy(view, view, sem).wait()

    def spread(buffer, index, which, peers):
        for peer in peers:
            remote(buffer.at[index], buffer.at[index], which, peer).start()

    load_w.wait()
    load_f.wait()

    before = None
    for i in range(B):
        w = warmth[i]
        c = conductivity(w, factor[i])
        h = half_resistance(c)
        half_x[i] = h
        warmth_t[pl.ds(i, B, stride=B), :] = w
        conduct_t[pl.ds(i, B, stride=B), :] = c
        half_y[pl.ds(i, B, stride=B), :] = h
        if before is None:
            edge_low_c = c
            flux_low = None
        else:
            flux_high = inverse(before[1] + h) * (w - before[0])
            gain = flux_high if flux_low is None else flux_high - flux_low
            side_t[pl.ds(i - 1, B, stride=B), :] = gain
            flux_low = flux_high
        before = (w, h)
    side_t[pl.ds(B - 1, B, stride=B), :] = -flux_low
    edge_high_c = c

    class Rows:
        def __init__(self, ref):
            self.ref = ref

        def __getitem__(self, i):
            return self.ref[i * B : (i + 1) * B, :]

    half_rows = Rows(half_y)
    block_coefficients(half_rows, link_y, back_y, gf_y, gl_y, co_z.at[me_z])
    spread(co_z, me_z, 1, z_peers)

    flux_low = None
    for i in range(B):
        if i < B - 1:
            flux_high = inverse(half_rows[i] + half_rows[i + 1]) * (
                warmth_t[(i + 1) * B : (i + 2) * B, :] - warmth_t[i * B : (i + 1) * B, :]
            )
        gain = flux_high if i == 0 else (-flux_low if i == B - 1 else flux_high - flux_low)
        side_t[i * B : (i + 1) * B, :] = side_t[i * B : (i + 1) * B, :] + gain
        flux_low = flux_high

    lane = lax.broadcasted_iota(jnp.int32, (64, NZ), 1)

    def upright(n, carry):
        rows = pl.ds(pl.multiple_of(n * 64, 64), 64)
        w = warmth_t[rows, :]
        c = conduct_t[rows, :]
        link, main = upright_bands(c, lane)
        lower = UPRIGHT * c * (w - WARM_WALL)
        flux = jnp.where(lane == 0, lower, link * (w - up(w, 1)))
        upper = UPRIGHT * c * (CHILL_WALL - w)
        flux_above = jnp.where(lane == NZ - 1, upper, down(flux, 1))
        side = 2.0 * (side_t[rows, :] + (flux_above - flux))
        for stride in STEPS:
            low, high, link, main = upright_step(link, main, stride)
            side = side + low * up(side, stride) + down(high * side, stride)
        side_t[rows, :] = side * inverse(main)
        return carry

    lax.fori_loop(0, 4, upright, 0)

    last = B * (B - 1)
    edge_c = jnp.concatenate(
        [edge_low_c, edge_high_c, conduct_t[0:B, :], conduct_t[last : last + B, :]], axis=0
    )
    link, main = upright_bands(edge_c, lane)
    for n, stride in enumerate(STEPS):
        low, high, link, main = upright_step(link, main, stride)
        low_f[n] = low
        high_f[n] = high
    scale_f[...] = inverse(main)

    settle(halo, 8, recv_sem.at[0])

    def through(near_w, near_h, k, present):
        other = halo[k]
        resist = near_h + half_resistance(conductivity(other, halo[k + 1]))
        return (2.0 * present) * (inverse(resist) * (other - near_w))

    def flag(condition):
        return jnp.where(condition, 1.0, 0.0).astype(jnp.float32)

    share = jnp.concatenate(
        [
            through(warmth[0], half_x[0], 0, flag(row > 0)),
            through(warmth[B - 1], half_x[B - 1], 2, flag(row < ROWS - 1)),
            through(warmth_t[0:B, :], half_rows[0], 4, flag(col > 0)),
            through(warmth_t[last : last + B, :], half_rows[B - 1], 6, flag(col < columns - 1)),
        ],
        axis=0,
    )
    for n, stride in enumerate(STEPS):
        share = share + low_f[n] * up(share, stride) + down(high_f[n] * share, stride)
    share = share * scale_f[...]
    side_t[0:B, :] = side_t[0:B, :] + share[2 * B : 3 * B]
    side_t[last : last + B, :] = side_t[last : last + B, :] + share[3 * B : 4 * B]
    side_t[pl.ds(0, B, stride=B), :] = side_t[pl.ds(0, B, stride=B), :] + share[0:B]
    side_t[pl.ds(B - 1, B, stride=B), :] = side_t[pl.ds(B - 1, B, stride=B), :] + share[B : 2 * B]

    side_rows = Rows(side_t)
    block_ends(lambda i: side_rows[i], gf_y, gl_y, end_z.at[me_z])
    spread(end_z, me_z, 2, z_peers)

    settle(co_z, GROUP - 1, recv_sem.at[1])
    chain_factors(GROUP, co_z, ch_link.at[0], ch_inv.at[0], ch_carry.at[0])
    group_coefficients(
        co_z, ch_link.at[0], ch_inv.at[0], ch_carry.at[0], from_left, from_right, co_x.at[me_x]
    )
    spread(co_x, me_x, 3, x_peers)
    block_coefficients(half_x, link_x, back_x, gf_x, gl_x, co_r.at[row])
    spread(co_r, row, 4, row_peers)

    def keep(i, value):
        solved[i] = value

    block_solve(lambda i: side_rows[i], keep, link_y, back_y, gl_y)
    zero = jnp.zeros((B, NZ), jnp.float32)
    for ref, count in ((flux_z, GROUP), (flux_x, GROUPS), (flux_r, ROWS)):
        ref[0] = zero
        ref[count] = zero

    settle(end_z, GROUP - 1, recv_sem.at[2])
    chain_solve(GROUP, end_z, ch_link.at[0], ch_inv.at[0], ch_carry.at[0], flux_z)
    end_x[me_x, 0] = end_z[0, 0] + co_z[0, 2] * flux_z[1]
    end_x[me_x, 1] = end_z[GROUP - 1, 1] - co_z[GROUP - 1, 2] * flux_z[GROUP - 1]
    spread(end_x, me_x, 5, x_peers)

    settle(co_x, GROUPS - 1, recv_sem.at[3])
    chain_factors(GROUPS, co_x, ch_link.at[1], ch_inv.at[1], ch_carry.at[1])
    settle(co_r, ROWS - 1, recv_sem.at[4])
    chain_factors(ROWS, co_r, ch_link.at[2], ch_inv.at[2], ch_carry.at[2])

    settle(end_x, GROUPS - 1, recv_sem.at[5])
    chain_solve(GROUPS, end_x, ch_link.at[1], ch_inv.at[1], ch_carry.at[1], flux_x)
    outer_low, outer_high = flux_x[me_x], flux_x[me_x + 1]

    def inner_flux(i):
        return flux_z[i] + from_left[i] * outer_low + from_right[i] * outer_high

    flux_low, flux_high = inner_flux(me_z), inner_flux(me_z + 1)
    for i in range(B):
        side_n[pl.ds(i, B, stride=B), :] = solved[i] - gf_y[i] * flux_low + gl_y[i] * flux_high

    section = Rows(side_n)
    block_ends(lambda i: section[i], gf_x, gl_x, end_r.at[row])
    spread(end_r, row, 6, row_peers)
    block_solve(lambda i: section[i], keep, link_x, back_x, gl_x)

    settle(end_r, ROWS - 1, recv_sem.at[6])
    chain_solve(ROWS, end_r, ch_link.at[2], ch_inv.at[2], ch_carry.at[2], flux_r)
    flux_low, flux_high = flux_r[row], flux_r[row + 1]
    for i in range(B):
        out_ref[i] = warmth[i] + (solved[i] - gf_x[i] * flux_low + gl_x[i] * flux_high)

    settle(halo, 8, send_sem.at[0])
    settle(co_z, GROUP - 1, send_sem.at[1])
    settle(end_z, GROUP - 1, send_sem.at[2])
    settle(co_x, GROUPS - 1, send_sem.at[3])
    settle(co_r, ROWS - 1, send_sem.at[4])
    settle(end_x, GROUPS - 1, send_sem.at[5])
    settle(end_r, ROWS - 1, send_sem.at[6])


def shards(warmth, factor):
    def vmem(*shape):
        return pltpu.VMEM(shape, jnp.float32)

    scratch = [
        vmem(B, B, NZ),
        vmem(B, B, NZ),
        vmem(B, B, NZ),
        vmem(B * B, NZ),
        vmem(B * B, NZ),
        vmem(B * B, NZ),
        vmem(B * B, NZ),
        vmem(B * B, NZ),
        vmem(8, B, NZ),
        vmem(len(STEPS), 4 * B, NZ),
        vmem(len(STEPS), 4 * B, NZ),
        vmem(4 * B, NZ),
    ]
    scratch += [vmem(B, B, NZ) for _ in range(8)]
    scratch += [
        vmem(B, B, NZ),
        vmem(GROUP, 3, B, NZ),
        vmem(GROUPS, 3, B, NZ),
        vmem(ROWS, 3, B, NZ),
        vmem(GROUP, 2, B, NZ),
        vmem(GROUPS, 2, B, NZ),
        vmem(ROWS, 2, B, NZ),
        vmem(3, GROUP, B, NZ),
        vmem(3, GROUP, B, NZ),
        vmem(3, GROUP, B, NZ),
        vmem(GROUP + 1, B, NZ),
        vmem(GROUPS + 1, B, NZ),
        vmem(ROWS + 1, B, NZ),
        vmem(GROUP + 1, B, NZ),
        vmem(GROUP + 1, B, NZ),
        pltpu.SemaphoreType.DMA((2,)),
        pltpu.SemaphoreType.DMA((7,)),
        pltpu.SemaphoreType.DMA((7,)),
    ]
    return pl.pallas_call(
        kernel,
        out_shape=jax.ShapeDtypeStruct((B, B, NZ), jnp.float32),
        in_specs=[pl.BlockSpec(memory_space=pl.ANY)] * 2,
        out_specs=pl.BlockSpec(memory_space=pltpu.VMEM),
        scratch_shapes=scratch,
        compiler_params=pltpu.CompilerParams(
            collective_id=0, has_side_effects=True, vmem_limit_bytes=48 * 2**20
        ),
    )(warmth, factor)


def solution(mesh):
    return jax.shard_map(
        shards,
        mesh=mesh,
        in_specs=(P("row", "col", None), P("row", "col", None)),
        out_specs=P("row", "col", None),
        check_vma=False,
    )
```

time: 168 us -> 30.8 us (0.18)
  waiting for transfers between devices: 80.3 us -> 0 us
  Pallas kernels: 0 us -> 28.2 us
  local copies, waits for them, and re-layouts: 24.9 us -> 2.47 us
  blocking collectives: 17.8 us -> 0 us
  other arithmetic: 17.6 us -> 0 us
  between operations: 15.5 us -> 0.01 us
  starting transfers between devices: 12 us -> 0 us
    all_gather x1 -> x0, waiting for transfers between devices: 78 us -> none  [settle_y(): everyone = lax.all_gather(packed[None], 'col', axis=0, tiled=True)]
    pallas_call x0 -> x1, Pallas kernels: none -> 28.2 us  [shards(): pl.pallas_call(kernel, out_shape=jax.ShapeDtypeStruct((B, B, NZ), jnp.flo...]
    slice x165 -> x0, local copies, waits for them, and re-layouts: 21.1 us -> none  [the longest x67 15.3 us: shifted_up(): kept_part = lax.slice_in_dim(values, stride, length, axis=dimension)]
    all_gather x1 -> x0, blocking collectives: 17.8 us -> none  [settle_x(): everyone = lax.all_gather(packed[None], 'row', axis=0, tiled=True)]
    add x60 -> x0, other arithmetic: 13.4 us -> none  [the longest x9 3.07 us: solve_chain(): rhs_vec = tuple((r + a + b for r, a, b in zip(rhs_vec, add_one, add_two)))]
    ppermute x4 -> x0, starting transfers between devices: 12 us -> none  [the longest x2 8.75 us: padded(): lax.ppermute(tail, axis, [(i, (i + 1) % count) for i in range(ends)])]
    ppermute x4 -> x0, waiting for transfers between devices: 2.31 us -> none  [the longest x2 1.53 us: padded(): lax.ppermute(head, axis, [((i + 1) % count, i) for i in range(ends)])]
  transfers between devices with their start and end apart: 5 -> 0, of which waited for: 3 -> 0; matrix products, arithmetic and copies ran while one was open for 1% -> 0% of each run, Pallas kernels for 0% -> 0%
where the time goes in v1:
time: 30.8 us; the launch traced here: 30.7 us
  Pallas kernels  28.2 us (92%)
  local copies, waits for them, and re-layouts  2.47 us (8%)
    pallas_call x1, Pallas kernels, shards(): pl.pallas_call(kernel, out_shape=jax.ShapeDtypeStruct((B, B, NZ), jnp.flo...  28.2 us
    unnamed x5, local copies, waits for them, and re-layouts  2.47 us

profile of v1, /device:TPU:1, one launch (start us, length us, event | category | flops | bytes accessed | tf_op | source)
XLA Modules:
  0.0 30.7 jit_solution(6331132180446647817)
XLA Ops:
  0.0 0.0 copy-start
  0.0 0.9 %copy-done = f32[16,16,128]{2,1,0:T(8,128)S(1)} copy-done((f32[16,16,128]{2,1,0:T(8,128)S(1)}, f32[16,16,128]{2,1,0:T(8,128)}, u32[]{:S(2)}) %copy-start) | copy-done | bytes 131096
  0.9 0.0 copy-start.1
  0.9 0.9 %copy-done.1 = f32[16,16,128]{2,1,0:T(8,128)S(1)} copy-done((f32[16,16,128]{2,1,0:T(8,128)S(1)}, f32[16,16,128]{2,1,0:T(8,128)}, u32[]{:S(2)}) %copy-start.1) | copy-done | bytes 131096
  1.8 28.2 %shard_map.28 = f32[16,16,128]{2,1,0:T(8,128)S(1)} custom-call(f32[16,16,128]{2,1,0:T(8,128)S(1)} %copy-done, f32[16,16,128]{2,1,0:T(8,128)S(1)} %copy-done.1), custom_call_target="tpu_custom_call" | custom-call | tf_op jit(solution)/shard_map/pallas_call | solution.py:459
  30.0 0.7 %copy.4 = f32[16,16,128]{2,1,0:T(8,128)} copy(f32[16,16,128]{2,1,0:T(8,128)S(1)} %shard_map.28) | data formatting | bytes 262144
Async XLA Ops:
  0.0 0.9 %copy-start = (f32[16,16,128]{2,1,0:T(8,128)S(1)}, f32[16,16,128]{2,1,0:T(8,128)}, u32[]{:S(2)}) copy-start(f32[16,16,128]{2,1,0:T(8,128)} %warmth_hbm.1) | copy-start | bytes 393220
  0.9 0.9 %copy-start.1 = (f32[16,16,128]{2,1,0:T(8,128)S(1)}, f32[16,16,128]{2,1,0:T(8,128)}, u32[]{:S(2)}) copy-start(f32[16,16,128]{2,1,0:T(8,128)} %factor_hbm.1) | copy-start | bytes 393220

commit v2 on v1

--- a/solution.py
+++ b/solution.py
@@ -19,6 +19,7 @@
 GROUP = 8
 GROUPS = 4
 STEPS = (1, 2, 4, 8, 16, 32, 64)
+WEIGHTS = 19
 
 
 def inverse(value):
@@ -142,7 +143,8 @@
     return pltpu.roll(value, NZ - stride, axis=1)
 
 
-def upright_bands(conduct, lane):
+def upright_bands(conduct):
+    lane = lax.broadcasted_iota(jnp.int32, conduct.shape, 1)
     below = up(conduct, 1)
     face = (2.0 * conduct * below) * inverse(conduct + below)
     inner = jnp.where(lane == 0, 0.0, UPRIGHT * face)
@@ -172,8 +174,7 @@
     side_t,
     side_n,
     halo,
-    low_f,
-    high_f,
+    weights,
     scale_f,
     link_x,
     back_x,
@@ -295,36 +296,38 @@
         side_t[i * B : (i + 1) * B, :] = side_t[i * B : (i + 1) * B, :] + gain
         flux_low = flux_high
 
-    lane = lax.broadcasted_iota(jnp.int32, (64, NZ), 1)
-
-    def upright(n, carry):
-        rows = pl.ds(pl.multiple_of(n * 64, 64), 64)
-        w = warmth_t[rows, :]
-        c = conduct_t[rows, :]
-        link, main = upright_bands(c, lane)
-        lower = UPRIGHT * c * (w - WARM_WALL)
-        flux = jnp.where(lane == 0, lower, link * (w - up(w, 1)))
-        upper = UPRIGHT * c * (CHILL_WALL - w)
-        flux_above = jnp.where(lane == NZ - 1, upper, down(flux, 1))
-        side = 2.0 * (side_t[rows, :] + (flux_above - flux))
-        for stride in STEPS:
-            low, high, link, main = upright_step(link, main, stride)
-            side = side + low * up(side, stride) + down(high * side, stride)
-        side_t[rows, :] = side * inverse(main)
-        return carry
-
-    lax.fori_loop(0, 4, upright, 0)
-
-    last = B * (B - 1)
-    edge_c = jnp.concatenate(
-        [edge_low_c, edge_high_c, conduct_t[0:B, :], conduct_t[last : last + B, :]], axis=0
-    )
-    link, main = upright_bands(edge_c, lane)
-    for n, stride in enumerate(STEPS):
+    cells, last = B * B, B * (B - 1)
+    lane = lax.broadcasted_iota(jnp.int32, (cells, NZ), 1)
+    w = warmth_t[...]
+    c = conduct_t[...]
+    link, main = upright_bands(jnp.concatenate([c, edge_low_c, edge_high_c], axis=0))
+    flux = jnp.where(lane == 0, UPRIGHT * c * (w - WARM_WALL), link[0:cells] * (w - up(w, 1)))
+    flux_above = jnp.where(lane == NZ - 1, UPRIGHT * c * (CHILL_WALL - w), down(flux, 1))
+    side = 2.0 * (side_t[...] + (flux_above - flux))
+
+    def faces(value):
+        return jnp.concatenate(
+            [value[cells : cells + 2 * B], value[0:B], value[last : last + B]], axis=0
+        )
+
+    lows, highs = [], []
+    for stride in STEPS:
         low, high, link, main = upright_step(link, main, stride)
-        low_f[n] = low
-        high_f[n] = high
-    scale_f[...] = inverse(main)
+        side = side + low[0:cells] * up(side, stride) + down(high[0:cells] * side, stride)
+        lows.append(faces(low))
+        highs.append(down(faces(high), stride))
+    inv = inverse(main)
+    side_t[...] = side * inv[0:cells]
+    scale_f[...] = faces(inv)
+    for n in range(0, len(STEPS) - 1, 2):
+        wide = STEPS[n + 1]
+        weights[3 * n] = lows[n] + lows[n + 1] * up(highs[n], wide)
+        weights[3 * n + 1] = highs[n] + highs[n + 1] * down(lows[n], wide)
+        weights[3 * n + 2] = lows[n + 1]
+        weights[3 * n + 3] = highs[n + 1]
+        weights[3 * n + 4] = lows[n + 1] * up(lows[n], wide)
+        weights[3 * n + 5] = highs[n + 1] * down(highs[n], wide)
+    weights[WEIGHTS - 1] = lows[-1] + highs[-1]
 
     settle(halo, 8, recv_sem.at[0])
 
@@ -345,9 +348,15 @@
         ],
         axis=0,
     )
-    for n, stride in enumerate(STEPS):
-        share = share + low_f[n] * up(share, stride) + down(high_f[n] * share, stride)
-    share = share * scale_f[...]
+    for n in range(0, len(STEPS) - 1, 2):
+        stride = STEPS[n]
+        share = (
+            (share + weights[3 * n] * up(share, stride))
+            + (weights[3 * n + 1] * down(share, stride) + weights[3 * n + 2] * up(share, 2 * stride))
+            + (weights[3 * n + 3] * down(share, 2 * stride) + weights[3 * n + 4] * up(share, 3 * stride))
+            + weights[3 * n + 5] * down(share, 3 * stride)
+        )
+    share = (share + weights[WEIGHTS - 1] * up(share, STEPS[-1])) * scale_f[...]
     side_t[0:B, :] = side_t[0:B, :] + share[2 * B : 3 * B]
     side_t[last : last + B, :] = side_t[last : last + B, :] + share[3 * B : 4 * B]
     side_t[pl.ds(0, B, stride=B), :] = side_t[pl.ds(0, B, stride=B), :] + share[0:B]
@@ -431,8 +440,7 @@
         vmem(B * B, NZ),
         vmem(B * B, NZ),
         vmem(8, B, NZ),
-        vmem(len(STEPS), 4 * B, NZ),
-        vmem(len(STEPS), 4 * B, NZ),
+        vmem(WEIGHTS, 4 * B, NZ),
         vmem(4 * B, NZ),
     ]
     scratch += [vmem(B, B, NZ) for _ in range(8)]
@@ -459,11 +467,11 @@
     return pl.pallas_call(
         kernel,
         out_shape=jax.ShapeDtypeStruct((B, B, NZ), jnp.float32),
-        in_specs=[pl.BlockSpec(memory_space=pl.ANY)] * 2,
+        in_specs=[pl.BlockSpec(memory_space=pltpu.HBM)] * 2,
         out_specs=pl.BlockSpec(memory_space=pltpu.VMEM),
         scratch_shapes=scratch,
         compiler_params=pltpu.CompilerParams(
-            collective_id=0, has_side_effects=True, vmem_limit_bytes=48 * 2**20
+            collective_id=0, has_side_effects=True, vmem_limit_bytes=55040 * 1024
         ),
     )(warmth, factor)
 

time: 30.8 us -> 29.1 us (0.945)
  local copies, waits for them, and re-layouts: 2.47 us -> 0.66 us
    unnamed x5 -> x1, local copies, waits for them, and re-layouts: 2.47 us -> 0.66 us
where the time goes in v2:
time: 29.1 us; the launch traced here: 29 us
  Pallas kernels  28.4 us (98%)
  local copies, waits for them, and re-layouts  0.66 us (2%)
    pallas_call x1, Pallas kernels, shards(): pl.pallas_call(kernel, out_shape=jax.ShapeDtypeStruct((B, B, NZ), jnp.flo...  28.4 us
    unnamed x1, local copies, waits for them, and re-layouts  0.66 us

profile of v2, /device:TPU:1, one launch (start us, length us, event | category | flops | bytes accessed | tf_op | source)
XLA Modules:
  0.0 29.0 jit_solution(3230470850551327067)
XLA Ops:
  0.0 28.4 %shard_map.28 = f32[16,16,128]{2,1,0:T(8,128)S(1)} custom-call(f32[16,16,128]{2,1,0:T(8,128)} %warmth_hbm.1, f32[16,16,128]{2,1,0:T(8,128)} %factor_hbm.1), custom_call_target="tpu_custom_call" | custom-call | tf_op jit(solution)/shard_map/pallas_call | solution.py:467
  28.4 0.7 %copy.4 = f32[16,16,128]{2,1,0:T(8,128)} copy(f32[16,16,128]{2,1,0:T(8,128)S(1)} %shard_map.28) | data formatting | bytes 262144

commit v3 on v2

--- a/solution.py
+++ b/solution.py
@@ -109,6 +109,41 @@
         out[i] = flux
 
 
+def two_sided_factors(count, coeffs, left_inv, right_inv, left_link, right_link):
+    zero = jnp.zeros((B, NZ), jnp.float32)
+    left_inv[0] = zero
+    right_inv[count] = zero
+    below, above = zero, zero
+    for i in range(1, count):
+        j = count - i
+        left_link[i - 1] = below
+        pivot = coeffs[i - 1, 1] + coeffs[i, 0] - coeffs[i - 1, 2] * below
+        pivot = inverse(pivot)
+        left_inv[i] = pivot
+        below = coeffs[i, 2] * pivot
+        right_link[j] = above
+        pivot = coeffs[j - 1, 1] + coeffs[j, 0] - coeffs[j, 2] * above
+        pivot = inverse(pivot)
+        right_inv[j] = pivot
+        above = coeffs[j - 1, 2] * pivot
+    left_link[count - 1] = below
+    right_link[0] = above
+
+
+def sweep_sides(count, parts, left_link, right_link, from_low, from_high):
+    zero = jnp.zeros((B, NZ), jnp.float32)
+    from_low[0] = zero
+    from_high[count] = zero
+    low, high = parts[0], parts[count - 1]
+    from_low[1] = low
+    from_high[count - 1] = high
+    for i in range(1, count - 1):
+        low = parts[i] + left_link[i] * low
+        from_low[i + 1] = low
+        high = parts[count - 1 - i] + right_link[count - 1 - i] * high
+        from_high[count - 1 - i] = high
+
+
 def group_coefficients(coeffs, link, inv, carry, from_left, from_right, out):
     n = GROUP
     zero = jnp.zeros((B, NZ), jnp.float32)
@@ -174,6 +209,7 @@
     side_t,
     side_n,
     halo,
+    edges,
     weights,
     scale_f,
     link_x,
@@ -196,7 +232,14 @@
     ch_carry,
     flux_z,
     flux_x,
-    flux_r,
+    ends,
+    parts,
+    left_inv,
+    right_inv,
+    left_link,
+    right_link,
+    from_low,
+    from_high,
     from_left,
     from_right,
     load_sem,
@@ -225,7 +268,13 @@
     load_f = pltpu.make_async_copy(factor_hbm, factor, load_sem.at[1])
     load_w.start()
     load_f.start()
-    pl.semaphore_wait(barrier, len(everyone))
+    load_w.wait()
+    load_f.wait()
+    for k, array in enumerate((warmth, factor)):
+        edges[0, k] = array[B - 1]
+        edges[1, k] = array[0]
+        edges[2, k] = array[:, B - 1, :]
+        edges[3, k] = array[:, 0, :]
 
     def remote(src, dst, which, peer):
         return pltpu.make_async_remote_copy(
@@ -237,11 +286,9 @@
             device_id_type=MESH,
         )
 
-    for k, array in enumerate((warmth_hbm, factor_hbm)):
-        remote(array.at[:, B - 1, :], halo.at[4 + k], 0, col_up).start()
-        remote(array.at[:, 0, :], halo.at[6 + k], 0, col_down).start()
-        remote(array.at[B - 1], halo.at[k], 0, row_up).start()
-        remote(array.at[0], halo.at[2 + k], 0, row_down).start()
+    pl.semaphore_wait(barrier, len(everyone))
+    for k, peer in enumerate((row_up, row_down, col_up, col_down)):
+        remote(edges.at[k], halo.at[k], 0, peer).start()
 
     def settle(buffer, count, sem):
         view = buffer.at[pl.ds(0, count)]
@@ -251,8 +298,6 @@
         for peer in peers:
             remote(buffer.at[index], buffer.at[index], which, peer).start()
 
-    load_w.wait()
-    load_f.wait()
 
     before = None
     for i in range(B):
@@ -329,11 +374,11 @@
         weights[3 * n + 5] = highs[n + 1] * down(highs[n], wide)
     weights[WEIGHTS - 1] = lows[-1] + highs[-1]
 
-    settle(halo, 8, recv_sem.at[0])
+    settle(halo, 4, recv_sem.at[0])
 
     def through(near_w, near_h, k, present):
-        other = halo[k]
-        resist = near_h + half_resistance(conductivity(other, halo[k + 1]))
+        other = halo[k, 0]
+        resist = near_h + half_resistance(conductivity(other, halo[k, 1]))
         return (2.0 * present) * (inverse(resist) * (other - near_w))
 
     def flag(condition):
@@ -342,9 +387,9 @@
     share = jnp.concatenate(
         [
             through(warmth[0], half_x[0], 0, flag(row > 0)),
-            through(warmth[B - 1], half_x[B - 1], 2, flag(row < ROWS - 1)),
-            through(warmth_t[0:B, :], half_rows[0], 4, flag(col > 0)),
-            through(warmth_t[last : last + B, :], half_rows[B - 1], 6, flag(col < columns - 1)),
+            through(warmth[B - 1], half_x[B - 1], 1, flag(row < ROWS - 1)),
+            through(warmth_t[0:B, :], half_rows[0], 2, flag(col > 0)),
+            through(warmth_t[last : last + B, :], half_rows[B - 1], 3, flag(col < columns - 1)),
         ],
         axis=0,
     )
@@ -380,7 +425,7 @@
 
     block_solve(lambda i: side_rows[i], keep, link_y, back_y, gl_y)
     zero = jnp.zeros((B, NZ), jnp.float32)
-    for ref, count in ((flux_z, GROUP), (flux_x, GROUPS), (flux_r, ROWS)):
+    for ref, count in ((flux_z, GROUP), (flux_x, GROUPS)):
         ref[0] = zero
         ref[count] = zero
 
@@ -393,7 +438,13 @@
     settle(co_x, GROUPS - 1, recv_sem.at[3])
     chain_factors(GROUPS, co_x, ch_link.at[1], ch_inv.at[1], ch_carry.at[1])
     settle(co_r, ROWS - 1, recv_sem.at[4])
-    chain_factors(ROWS, co_r, ch_link.at[2], ch_inv.at[2], ch_carry.at[2])
+    two_sided_factors(ROWS, co_r, left_inv, right_inv, left_link, right_link)
+    own_left, own_right, own_link = left_inv[row], right_inv[row + 1], co_r[row, 2]
+    to_high = own_link * own_left
+    to_low = own_link * own_right
+    weight_high = own_right * inverse(1.0 - to_high * to_low)
+    weight_cross = to_high * weight_high
+    weight_low = own_left * (1.0 + own_link * weight_cross)
 
     settle(end_x, GROUPS - 1, recv_sem.at[5])
     chain_solve(GROUPS, end_x, ch_link.at[1], ch_inv.at[1], ch_carry.at[1], flux_x)
@@ -407,17 +458,26 @@
         side_n[pl.ds(i, B, stride=B), :] = solved[i] - gf_y[i] * flux_low + gl_y[i] * flux_high
 
     section = Rows(side_n)
-    block_ends(lambda i: section[i], gf_x, gl_x, end_r.at[row])
-    spread(end_r, row, 6, row_peers)
+    block_ends(lambda i: section[i], gf_x, gl_x, ends)
+    own_first, own_last = ends[0], ends[1]
+    parts[0] = to_high * own_first - own_last
+    parts[1] = own_first - to_low * own_last
+    end_r[row] = own_first
+    for peer in row_peers:
+        side = jnp.where(peer[0] > row, 0, 1)
+        remote(parts.at[side], end_r.at[row], 6, peer).start()
     block_solve(lambda i: section[i], keep, link_x, back_x, gl_x)
 
     settle(end_r, ROWS - 1, recv_sem.at[6])
-    chain_solve(ROWS, end_r, ch_link.at[2], ch_inv.at[2], ch_carry.at[2], flux_r)
-    flux_low, flux_high = flux_r[row], flux_r[row + 1]
+    sweep_sides(ROWS, end_r, left_link, right_link, from_low, from_high)
+    low_side = own_first + from_low[row]
+    high_side = from_high[row + 1] - own_last
+    flux_low = weight_low * low_side + weight_cross * high_side
+    flux_high = weight_cross * low_side + weight_high * high_side
     for i in range(B):
         out_ref[i] = warmth[i] + (solved[i] - gf_x[i] * flux_low + gl_x[i] * flux_high)
 
-    settle(halo, 8, send_sem.at[0])
+    settle(halo, 4, send_sem.at[0])
     settle(co_z, GROUP - 1, send_sem.at[1])
     settle(end_z, GROUP - 1, send_sem.at[2])
     settle(co_x, GROUPS - 1, send_sem.at[3])
@@ -439,7 +499,8 @@
         vmem(B * B, NZ),
         vmem(B * B, NZ),
         vmem(B * B, NZ),
-        vmem(8, B, NZ),
+        vmem(4, 2, B, NZ),
+        vmem(4, 2, B, NZ),
         vmem(WEIGHTS, 4 * B, NZ),
         vmem(4 * B, NZ),
     ]
@@ -451,12 +512,19 @@
         vmem(ROWS, 3, B, NZ),
         vmem(GROUP, 2, B, NZ),
         vmem(GROUPS, 2, B, NZ),
-        vmem(ROWS, 2, B, NZ),
-        vmem(3, GROUP, B, NZ),
-        vmem(3, GROUP, B, NZ),
-        vmem(3, GROUP, B, NZ),
+        vmem(ROWS, B, NZ),
+        vmem(2, GROUP, B, NZ),
+        vmem(2, GROUP, B, NZ),
+        vmem(2, GROUP, B, NZ),
         vmem(GROUP + 1, B, NZ),
         vmem(GROUPS + 1, B, NZ),
+        vmem(2, B, NZ),
+        vmem(2, B, NZ),
+        vmem(ROWS + 1, B, NZ),
+        vmem(ROWS + 1, B, NZ),
+        vmem(ROWS, B, NZ),
+        vmem(ROWS, B, NZ),
+        vmem(ROWS + 1, B, NZ),
         vmem(ROWS + 1, B, NZ),
         vmem(GROUP + 1, B, NZ),
         vmem(GROUP + 1, B, NZ),

time: 29.1 us -> 28.5 us (0.979)
  Pallas kernels: 28.4 us -> 27.8 us
    pallas_call x1, Pallas kernels: 28.4 us -> 27.8 us  [shards(): pl.pallas_call(kernel, out_shape=jax.ShapeDtypeStruct((B, B, NZ), jnp.flo...]
where the time goes in v3:
time: 28.5 us; the launch traced here: 28.4 us
  Pallas kernels  27.8 us (98%)
  local copies, waits for them, and re-layouts  0.66 us (2%)
    pallas_call x1, Pallas kernels, shards(): pl.pallas_call(kernel, out_shape=jax.ShapeDtypeStruct((B, B, NZ), jnp.flo...  27.8 us
    unnamed x1, local copies, waits for them, and re-layouts  0.66 us

profile of v3, /device:TPU:1, one launch (start us, length us, event | category | flops | bytes accessed | tf_op | source)
XLA Modules:
  0.0 28.4 jit_solution(2002367236442410685)
XLA Ops:
  0.0 27.8 %shard_map.28 = f32[16,16,128]{2,1,0:T(8,128)S(1)} custom-call(f32[16,16,128]{2,1,0:T(8,128)} %warmth_hbm.1, f32[16,16,128]{2,1,0:T(8,128)} %factor_hbm.1), custom_call_target="tpu_custom_call" | custom-call | tf_op jit(solution)/shard_map/pallas_call | solution.py:535
  27.8 0.7 %copy.4 = f32[16,16,128]{2,1,0:T(8,128)} copy(f32[16,16,128]{2,1,0:T(8,128)S(1)} %shard_map.28) | data formatting | bytes 262144

commit v4 on v3

--- a/solution.py
+++ b/solution.py
@@ -287,7 +287,7 @@
         )
 
     pl.semaphore_wait(barrier, len(everyone))
-    for k, peer in enumerate((row_up, row_down, col_up, col_down)):
+    for k, peer in ((2, col_up), (3, col_down), (0, row_up), (1, row_down)):
         remote(edges.at[k], halo.at[k], 0, peer).start()
 
     def settle(buffer, count, sem):
@@ -329,7 +329,7 @@
 
     half_rows = Rows(half_y)
     block_coefficients(half_rows, link_y, back_y, gf_y, gl_y, co_z.at[me_z])
-    spread(co_z, me_z, 1, z_peers)
+    spread(co_z, me_z, 1, z_peers[::-1])
 
     flux_low = None
     for i in range(B):

time: 28.5 us -> 28.4 us (level)
  no operation moved by 1% of the time
where the time goes in v4:
time: 28.4 us; the launch traced here: 28.3 us
  Pallas kernels  27.6 us (97%)
  local copies, waits for them, and re-layouts  0.66 us (2%)
    pallas_call x1, Pallas kernels, shards(): pl.pallas_call(kernel, out_shape=jax.ShapeDtypeStruct((B, B, NZ), jnp.flo...  27.6 us
    unnamed x1, local copies, waits for them, and re-layouts  0.66 us

profile of v4, /device:TPU:1, one launch (start us, length us, event | category | flops | bytes accessed | tf_op | source)
XLA Modules:
  0.0 28.3 jit_solution(17663818797195711321)
XLA Ops:
  0.0 27.6 %shard_map.28 = f32[16,16,128]{2,1,0:T(8,128)S(1)} custom-call(f32[16,16,128]{2,1,0:T(8,128)} %warmth_hbm.1, f32[16,16,128]{2,1,0:T(8,128)} %factor_hbm.1), custom_call_target="tpu_custom_call" | custom-call | tf_op jit(solution)/shard_map/pallas_call | solution.py:535
  27.6 0.7 %copy.4 = f32[16,16,128]{2,1,0:T(8,128)} copy(f32[16,16,128]{2,1,0:T(8,128)S(1)} %shard_map.28) | data formatting | bytes 262144

commit v5 on v4

--- a/solution.py
+++ b/solution.py
@@ -418,7 +418,7 @@
     )
     spread(co_x, me_x, 3, x_peers)
     block_coefficients(half_x, link_x, back_x, gf_x, gl_x, co_r.at[row])
-    spread(co_r, row, 4, row_peers)
+    spread(co_r, row, 4, row_peers[::-1])
 
     def keep(i, value):
         solved[i] = value

time: 28.4 us -> 28.4 us (level)
  no operation moved by 1% of the time
where the time goes in v5:
time: 28.4 us; the launch traced here: 28.3 us
  Pallas kernels  27.6 us (97%)
  local copies, waits for them, and re-layouts  0.66 us (2%)
    pallas_call x1, Pallas kernels, shards(): pl.pallas_call(kernel, out_shape=jax.ShapeDtypeStruct((B, B, NZ), jnp.flo...  27.6 us
    unnamed x1, local copies, waits for them, and re-layouts  0.66 us

profile of v5, /device:TPU:1, one launch (start us, length us, event | category | flops | bytes accessed | tf_op | source)
XLA Modules:
  0.0 28.3 jit_solution(8926399154497213240)
XLA Ops:
  0.0 27.6 %shard_map.28 = f32[16,16,128]{2,1,0:T(8,128)S(1)} custom-call(f32[16,16,128]{2,1,0:T(8,128)} %warmth_hbm.1, f32[16,16,128]{2,1,0:T(8,128)} %factor_hbm.1), custom_call_target="tpu_custom_call" | custom-call | tf_op jit(solution)/shard_map/pallas_call | solution.py:535
  27.6 0.7 %copy.4 = f32[16,16,128]{2,1,0:T(8,128)} copy(f32[16,16,128]{2,1,0:T(8,128)S(1)} %shard_map.28) | data formatting | bytes 262144

commit v6 on v5

--- a/solution.py
+++ b/solution.py
@@ -260,14 +260,14 @@
     row_up, row_down = (lax.rem(row + 1, ROWS), col), (lax.rem(row + ROWS - 1, ROWS), col)
     col_up, col_down = (row, lax.rem(col + 1, columns)), (row, lax.rem(col + columns - 1, columns))
 
+    load_w = pltpu.make_async_copy(warmth_hbm, warmth, load_sem.at[0])
+    load_f = pltpu.make_async_copy(factor_hbm, factor, load_sem.at[1])
+    load_w.start()
+    load_f.start()
     barrier = pltpu.get_barrier_semaphore()
     everyone = [col_up, col_down] + row_peers + z_peers + x_peers
     for peer in everyone:
         pl.semaphore_signal(barrier, inc=1, device_id=peer, device_id_type=MESH)
-    load_w = pltpu.make_async_copy(warmth_hbm, warmth, load_sem.at[0])
-    load_f = pltpu.make_async_copy(factor_hbm, factor, load_sem.at[1])
-    load_w.start()
-    load_f.start()
     load_w.wait()
     load_f.wait()
     for k, array in enumerate((warmth, factor)):

time: 28.4 us -> 28.4 us (level)
  no operation moved by 1% of the time
where the time goes in v6:
time: 28.4 us; the launch traced here: 28.3 us
  Pallas kernels  27.7 us (98%)
  local copies, waits for them, and re-layouts  0.66 us (2%)
    pallas_call x1, Pallas kernels, shards(): pl.pallas_call(kernel, out_shape=jax.ShapeDtypeStruct((B, B, NZ), jnp.flo...  27.7 us
    unnamed x1, local copies, waits for them, and re-layouts  0.66 us

profile of v6, /device:TPU:1, one launch (start us, length us, event | category | flops | bytes accessed | tf_op | source)
XLA Modules:
  0.0 28.3 jit_solution(2728396077160876606)
XLA Ops:
  0.0 27.7 %shard_map.28 = f32[16,16,128]{2,1,0:T(8,128)S(1)} custom-call(f32[16,16,128]{2,1,0:T(8,128)} %warmth_hbm.1, f32[16,16,128]{2,1,0:T(8,128)} %factor_hbm.1), custom_call_target="tpu_custom_call" | custom-call | tf_op jit(solution)/shard_map/pallas_call | solution.py:535
  27.7 0.7 %copy.4 = f32[16,16,128]{2,1,0:T(8,128)} copy(f32[16,16,128]{2,1,0:T(8,128)S(1)} %shard_map.28) | data formatting | bytes 262144
